TPU v7x, 32 devices: a whole 2x2x4 slice. The times are simulated.
32 devices in a mesh: blk: 8 (over z, y), lag: 4 (over x, core).
Axes of the slice: x: 2, y: 2, z: 4, core: 2. Of those that a mesh axis runs over, the one named last changes fastest.
Arguments:
- seismograms: float32 [1024, 3, 1024], P(('blk', 'lag')), may hold values from -70 to 70
- onset_shift: int32 [1024], P(('blk', 'lag')), may hold values from 0 to 63
- start_bits: int32 [1024], P(('blk', 'lag')), may hold values from 0 to 65535
Outputs:
- embedding: float32 [16, 1024], P(None, ('blk', 'lag'))
Inputs may be any that keep to these rules, and one draw needn't show every extreme that they name: `start_bits`: bit k of an event's code is its entry in starting vector k.
All inputs are finite; a program needn't handle non-finite values.
Results may differ from a plain program's by a relative error of at most 0.0077.
Values may be sent and summed in bfloat16 or wider, within the bound.
A program may use at most 64 MiB of HBM per device.

v0:
```python
import jax
import jax.numpy as jnp
from jax import lax
from jax.sharding import PartitionSpec as P

SAMPLES = 1024
MAXLAG = 64
LAGS = 65
OFFMAX = 64
VECTORS = 16
ITERS = 3


sharpness = 64.0


def passed_along(value, axis, steps):
    count = lax.axis_size(axis)
    pairs = [(source, (source + steps) % count) for source in range(count)]
    return lax.ppermute(value, axis, pairs)


def align_unit(seismograms, onset_shift):
    padded = jnp.pad(seismograms, ((0, 0), (0, 0), (0, OFFMAX)))

    def slide(record, offset_at):
        return lax.dynamic_slice_in_dim(record, offset_at, SAMPLES, 1)

    aligned = jax.vmap(slide)(padded, onset_shift)
    energy = jnp.sum(aligned * aligned, axis=(1, 2))
    return (aligned * lax.rsqrt(energy + 1e-06)[:, None, None]).astype(jnp.bfloat16)


def neighbour_waves(unit_waves):
    centre = lax.all_gather(unit_waves, "lag", axis=0, tiled=True)
    beyond = passed_along(centre, "blk", -1)
    before = passed_along(centre, "blk", 1)
    blocks = (before, centre, beyond)
    return blocks


def neighbour_vectors(scaled):
    centre = lax.all_gather(scaled, "lag", axis=1, tiled=True)
    before = passed_along(centre, "blk", 1)
    beyond = passed_along(centre, "blk", -1)
    return jnp.concatenate((before, centre, beyond), 1)


def band_affinity(unit_waves, blocks):
    own_count = unit_waves.shape[0]
    flat_width = unit_waves.shape[1] * unit_waves.shape[2]
    padded = jnp.pad(unit_waves, ((0, 0), (0, 0), (MAXLAG, MAXLAG)))
    lag_group = 5
    flattened = [block.reshape(block.shape[0], flat_width) for block in blocks]

    def one_group(runnings, first_lag):
        shifted = jnp.concatenate(
            [
                lax.dynamic_slice_in_dim(
                    padded, 2 * MAXLAG - 2 * (first_lag + offset), SAMPLES, 2
                ).reshape(own_count, flat_width)
                for offset in range(lag_group)
            ],
            0,
        )
        updated = []
        for running, columns in zip(runnings, flattened):
            scores = lax.dot_general(
                shifted, columns, (((1,), (1,)), ((), ())), preferred_element_type=jnp.float32
            )
            weights = jnp.exp(sharpness * scores).reshape(lag_group, own_count, columns.shape[0])
            updated.append(running + jnp.sum(weights, axis=0))
        return (tuple(updated), None)

    starting = tuple(
        (jnp.zeros((own_count, columns.shape[0]), jnp.float32) for columns in flattened)
    )
    runnings, unused = lax.scan(
        one_group, starting, jnp.arange(0, LAGS, lag_group, dtype=jnp.int32)
    )
    return jnp.concatenate(runnings, 1)


def local(seismograms, onset_shift, start_bits):
    own_count = seismograms.shape[0]
    highest = lax.Precision.HIGHEST
    unit_waves = align_unit(seismograms, onset_shift)
    blocks = neighbour_waves(unit_waves)
    affinity = band_affinity(unit_waves, blocks)
    block_length = affinity.shape[1] // 3
    member = lax.axis_index("lag")
    column_ids = jnp.arange(3 * block_length, dtype=jnp.int32)
    self_ids = block_length + member * own_count + jnp.arange(own_count, dtype=jnp.int32)
    affinity = jnp.where(
        column_ids[None, :] == self_ids[:, None], jnp.zeros_like(affinity), affinity
    )
    degree = jnp.sum(affinity, axis=1)
    root_degree = jnp.sqrt(degree)
    inverse = lax.rsqrt(degree)
    events_all = own_count * lax.axis_size("blk") * lax.axis_size("lag")
    powers = 2 ** jnp.arange(VECTORS, dtype=jnp.int32)
    vectors = (start_bits[None, :] // powers[:, None] % 2).astype(jnp.float32)
    degree_total, projection = lax.psum(
        (jnp.sum(degree), jnp.dot(vectors, root_degree, precision=highest)), ("blk", "lag")
    )
    for iteration in range(ITERS):
        neighbours = neighbour_vectors(vectors * inverse)
        applied = lax.dot_general(neighbours, affinity, (((1,), (1,)), ((), ())), precision=highest)
        deflated = applied * inverse - root_degree * (projection / degree_total)[:, None]
        gram_local = jnp.dot(deflated, deflated.T, precision=highest)
        carried_local = jnp.dot(deflated, root_degree, precision=highest)
        gram_sum, carried = lax.psum((gram_local, carried_local), ("blk", "lag"))
        factor = jnp.linalg.cholesky(gram_sum / events_all)
        vectors = lax.linalg.triangular_solve(factor, deflated, left_side=True, lower=True)
        projection = lax.linalg.triangular_solve(
            factor, carried[:, None], left_side=True, lower=True
        )[:, 0]
    return vectors


def solution(mesh):
    return jax.shard_map(
        local,
        mesh=mesh,
        in_specs=(P(("blk", "lag"), None, None), P(("blk", "lag")), P(("blk", "lag"))),
        out_specs=P(None, ("blk", "lag")),
        check_vma=False,
    )
```

profile of v0, /device:TPU:0, one launch (start us, length us, event | category | flops | bytes accessed | tf_op | source)
XLA Modules:
  0.0 432.2 jit_solution(3291205660569676358)
XLA Ops:
  2.1 64.4 %while.19 = (s32[]{:T(128)}, f32[32,3,1088]{2,1,0:T(4,128)S(1)}, s32[32,3]{0,1:T(4,128)S(1)}, f32[32,3,1024]{2,1,0:T(4,128)S(1)}, s32[]{:T(128)}) while((s32[]{:T(128)}, f32[32,3,1088]{2,1,0:T(4,128)S(1)}, s32[32,3]{0,1:T(4,128)S(1)}, f32[32,3,1024]{2,1,0:T(4,128)S(1)}, s32[]{:T(128)}) %tuple.64), condition=%wide.while_cond, body=%wide.while_body.sunk | while | flops 2 | bytes 32893 | solution.py:27
  67.1 10.0 %all_gather.12 = bf16[128,3,1024]{2,0,1:T(8,128)(2,1)S(1)} all-gather(bf16[32,3,1024]{2,0,1:T(8,128)(2,1)S(1)} %fusion.12), channel_id=1, replica_groups=mesh['blk'=8,'lag'=4] {'lag'}, dimensions={0}, use_global_device_ids=true | all-gather | bytes 983040 | tf_op jit(solution)/shard_map/all_gather | solution.py:35
  77.5 4.6 %collective-permute-start.1 = (bf16[128,3,1024]{0,2,1:T(8,128)(2,1)S(1)}, bf16[128,3,1024]{0,2,1:T(8,128)(2,1)}, u32[]{:S(2)}, u32[]{:S(2)}) collective-permute-start(bf16[128,3,1024]{0,2,1:T(8,128)(2,1)S(1)} %copy.28), channel_id=1, source_target_pairs={{0,28},{4,0},{8,4},{12,8},{16,12},{20,16},{24,20},{28,24},{1,29},{... | collective-permute-start | bytes 2359304 | tf_op jit(solution)/shard_map/ppermute | solution.py:20
  83.5 30.8 %collective-permute-done.1 = bf16[128,3,1024]{0,2,1:T(8,128)(2,1)} collective-permute-done((bf16[128,3,1024]{0,2,1:T(8,128)(2,1)S(1)}, bf16[128,3,1024]{0,2,1:T(8,128)(2,1)}, u32[]{:S(2)}, u32[]{:S(2)}) %collective-permute-start.1) | collective-permute-done | bytes 786464 | tf_op jit(solution)/shard_map/ppermute | solution.py:20
  116.9 103.1 %while.20 = (s32[]{:T(128)}, f32[32,128]{1,0:T(8,128)S(1)}, f32[32,128]{1,0:T(8,128)S(1)}, f32[32,128]{1,0:T(8,128)S(1)}, s32[13]{0:T(128)S(1)}, /*index=5*/bf16...) while((s32[]{:T(128)}, f32[32,128]{1,0:T(8,128)S(1)}, ...), condition=%wide.region_5.6_spmd.clone, body=%wide.region_1.5_spmd.clone.sunk | while | flops 377622560 | bytes 15041106 | solution.py:78
  120.7 1.4 constant_dynamic-slice_fusion.9
  128.6 1.4 constant_dynamic-slice_fusion.9
  136.6 1.4 constant_dynamic-slice_fusion.9
  144.5 1.4 constant_dynamic-slice_fusion.9
  152.4 1.4 constant_dynamic-slice_fusion.9
  160.4 1.4 constant_dynamic-slice_fusion.9
  168.3 1.4 constant_dynamic-slice_fusion.9
  176.2 1.4 constant_dynamic-slice_fusion.9
  184.2 1.4 constant_dynamic-slice_fusion.9
  192.1 1.4 constant_dynamic-slice_fusion.9
  200.0 1.4 constant_dynamic-slice_fusion.9
  208.0 1.4 constant_dynamic-slice_fusion.9
  221.2 5.2 %all-gather = f32[4,32,16]{1,2,0:T(8,128)S(1)} all-gather(f32[1,32,16]{1,2,0:T(8,128)S(1)} %multiply_bitcast_fusion), channel_id=1, replica_groups=mesh['blk'=8,'lag'=4] {'lag'}, dimensions={0}, use_global_device_ids=true | all-gather | bytes 10240 | tf_op jit(solution)/shard_map/all_gather | solution.py:43
  226.5 3.2 collective-permute-start.3
  229.7 39.9 %all-reduce.5 = (f32[16]{0:T(128)S(1)}, f32[]{:T(128)}) all-reduce(f32[16]{0:T(128)S(1)} %convolution_bitcast_fusion.4, f32[]{:T(128)} %get-tuple-element.209), channel_id=1, replica_groups=mesh['blk'=8,'lag'=4] {'blk','lag'}, use_global_device_ids=true, to_apply=%region_7.8 | all-reduce | flops 17 | bytes 136 | tf_op jit(solution)/shard_map/psum | solution.py:103
  270.7 41.3 %all-reduce.4 = (f32[16,16]{0,1:T(8,128)S(1)}, f32[16,1]{0,1:T(1,128)S(1)}) all-reduce(f32[16,16]{0,1:T(8,128)S(1)} %fusion.69, f32[16,1]{0,1:T(1,128)S(1)} %convolution_bitcast_fusion.3), channel_id=1, replica_groups=mesh['blk'=8,'lag'=4] {'blk','lag'}, use_global_device_ids=true, to_apply=%region_10.11 | all-reduce | flops 272 | bytes 2176 | tf_op jit(solution)/shard_map/psum | solution.py:112
  312.2 1.5 cholesky.59
  316.5 5.5 %all-gather.1 = f32[4,32,16]{1,2,0:T(8,128)S(1)} all-gather(f32[1,32,16]{1,2,0:T(8,128)S(1)} %fusion.6), channel_id=1, replica_groups=mesh['blk'=8,'lag'=4] {'lag'}, dimensions={0}, use_global_device_ids=true | all-gather | bytes 10240 | tf_op jit(solution)/shard_map/all_gather | solution.py:43
  322.1 3.7 collective-permute-start.5
  327.2 5.0 %collective-permute-done.4 = f32[16,128]{1,0:T(8,128)S(1)} collective-permute-done((f32[16,128]{1,0:T(8,128)S(1)}, f32[16,128]{1,0:T(8,128)S(1)}, u32[]{:S(2)}, u32[]{:S(2)}) %collective-permute-start.4) | collective-permute-done | bytes 8224 | tf_op jit(solution)/shard_map/ppermute | solution.py:20
  332.7 37.0 %all-reduce.3 = (f32[16,16]{0,1:T(8,128)S(1)}, f32[16,1]{0,1:T(1,128)S(1)}) all-reduce(f32[16,16]{0,1:T(8,128)S(1)} %fusion.70, f32[16,1]{0,1:T(1,128)S(1)} %convolution_bitcast_fusion.1), channel_id=1, replica_groups=mesh['blk'=8,'lag'=4] {'blk','lag'}, use_global_device_ids=true, to_apply=%region_14.18 | all-reduce | flops 272 | bytes 2176 | tf_op jit(solution)/shard_map/psum | solution.py:112
  369.8 1.5 cholesky.70
  374.1 5.5 %all-gather.2 = f32[4,32,16]{1,2,0:T(8,128)S(1)} all-gather(f32[1,32,16]{1,2,0:T(8,128)S(1)} %fusion.4), channel_id=1, replica_groups=mesh['blk'=8,'lag'=4] {'lag'}, dimensions={0}, use_global_device_ids=true | all-gather | bytes 10240 | tf_op jit(solution)/shard_map/all_gather | solution.py:43
  379.7 3.7 collective-permute-start.7
  384.8 5.0 %collective-permute-done.6 = f32[16,128]{1,0:T(8,128)S(1)} collective-permute-done((f32[16,128]{1,0:T(8,128)S(1)}, f32[16,128]{1,0:T(8,128)S(1)}, u32[]{:S(2)}, u32[]{:S(2)}) %collective-permute-start.6) | collective-permute-done | bytes 8224 | tf_op jit(solution)/shard_map/ppermute | solution.py:20
  390.1 37.2 %psum.55 = f32[16,16]{0,1:T(8,128)S(1)} all-reduce(f32[16,16]{0,1:T(8,128)S(1)} %fusion.71), channel_id=1, replica_groups=mesh['blk'=8,'lag'=4] {'blk','lag'}, use_global_device_ids=true, to_apply=%region_16.20 | all-reduce | flops 256 | bytes 2048 | tf_op jit(solution)/shard_map/psum | solution.py:112
  427.4 1.5 cholesky.81
  (450 shorter events, 129.4 us)
Async XLA Ops:
  0.0 0.7 copy-start.2
  77.5 36.8 %collective-permute-start.1 = (bf16[128,3,1024]{0,2,1:T(8,128)(2,1)S(1)}, bf16[128,3,1024]{0,2,1:T(8,128)(2,1)}, u32[]{:S(2)}, u32[]{:S(2)}) collective-permute-start(bf16[128,3,1024]{0,2,1:T(8,128)(2,1)S(1)} %copy.28), channel_id=1, source_target_pairs={{0,28},{4,0},{8,4},{12,8},{16,12},{20,16},{24,20},{28,24},{1,29},{... | collective-permute-start | bytes 2359304 | tf_op jit(solution)/shard_map/ppermute | solution.py:20
  82.1 33.6 %collective-permute-start = (bf16[128,3,1024]{0,2,1:T(8,128)(2,1)S(1)}, bf16[128,3,1024]{0,2,1:T(8,128)(2,1)S(1)}, u32[]{:S(2)}, u32[]{:S(2)}) collective-permute-start(bf16[128,3,1024]{0,2,1:T(8,128)(2,1)S(1)} %copy.28), channel_id=1, source_target_pairs={{0,4},{4,8},{8,12},{12,16},{16,20},{20,24},{24,28},{28,0},{1,5},{5... | collective-permute-start | bytes 2359304 | tf_op jit(solution)/shard_map/ppermute | solution.py:20
  82.3 0.7 copy-start.1
  123.1 1.1 copy-start
  131.1 1.1 copy-start
  139.0 1.1 copy-start
  146.9 1.1 copy-start
  154.9 1.1 copy-start
  162.8 1.1 copy-start
  170.7 1.1 copy-start
  178.7 1.1 copy-start
  186.6 1.1 copy-start
  194.5 1.1 copy-start
  202.5 1.1 copy-start
  210.4 1.1 copy-start
  218.3 1.1 copy-start
  226.5 43.7 %collective-permute-start.3 = (f32[16,128]{1,0:T(8,128)S(1)}, f32[16,128]{1,0:T(8,128)S(1)}, u32[]{:S(2)}, u32[]{:S(2)}) collective-permute-start(f32[16,128]{1,0:T(8,128)S(1)} %bitcast.222), channel_id=1, source_target_pairs={{0,28},{4,0},{8,4},{12,8},{16,12},{20,16},{24,20},{28,24},{1,29},{... | collective-permute-start | bytes 24584 | tf_op jit(solution)/shard_map/ppermute | solution.py:20
  229.7 40.6 %collective-permute-start.2 = (f32[16,128]{1,0:T(8,128)S(1)}, f32[16,128]{1,0:T(8,128)S(1)}, u32[]{:S(2)}, u32[]{:S(2)}) collective-permute-start(f32[16,128]{1,0:T(8,128)S(1)} %bitcast.223), channel_id=1, source_target_pairs={{0,4},{4,8},{8,12},{12,16},{16,20},{20,24},{24,28},{28,0},{1,5},{5... | collective-permute-start | bytes 24584 | tf_op jit(solution)/shard_map/ppermute | solution.py:20
  322.1 5.1 %collective-permute-start.5 = (f32[16,128]{1,0:T(8,128)S(1)}, f32[16,128]{1,0:T(8,128)S(1)}, u32[]{:S(2)}, u32[]{:S(2)}) collective-permute-start(f32[16,128]{1,0:T(8,128)S(1)} %bitcast.225), channel_id=1, source_target_pairs={{0,28},{4,0},{8,4},{12,8},{16,12},{20,16},{24,20},{28,24},{1,29},{... | collective-permute-start | bytes 24584 | tf_op jit(solution)/shard_map/ppermute | solution.py:20
  325.8 6.3 %collective-permute-start.4 = (f32[16,128]{1,0:T(8,128)S(1)}, f32[16,128]{1,0:T(8,128)S(1)}, u32[]{:S(2)}, u32[]{:S(2)}) collective-permute-start(f32[16,128]{1,0:T(8,128)S(1)} %bitcast.226), channel_id=1, source_target_pairs={{0,4},{4,8},{8,12},{12,16},{16,20},{20,24},{24,28},{28,0},{1,5},{5... | collective-permute-start | bytes 24584 | tf_op jit(solution)/shard_map/ppermute | solution.py:20
  379.7 5.1 %collective-permute-start.7 = (f32[16,128]{1,0:T(8,128)S(1)}, f32[16,128]{1,0:T(8,128)S(1)}, u32[]{:S(2)}, u32[]{:S(2)}) collective-permute-start(f32[16,128]{1,0:T(8,128)S(1)} %bitcast.219), channel_id=1, source_target_pairs={{0,28},{4,0},{8,4},{12,8},{16,12},{20,16},{24,20},{28,24},{1,29},{... | collective-permute-start | bytes 24584 | tf_op jit(solution)/shard_map/ppermute | solution.py:20
  383.4 6.3 %collective-permute-start.6 = (f32[16,128]{1,0:T(8,128)S(1)}, f32[16,128]{1,0:T(8,128)S(1)}, u32[]{:S(2)}, u32[]{:S(2)}) collective-permute-start(f32[16,128]{1,0:T(8,128)S(1)} %bitcast.220), channel_id=1, source_target_pairs={{0,4},{4,8},{8,12},{12,16},{16,20},{20,24},{24,28},{28,0},{1,5},{5... | collective-permute-start | bytes 24584 | tf_op jit(solution)/shard_map/ppermute | solution.py:20
where the time goes:
time: 435 us; the launch traced here: 432 us
  blocking collectives  182 us (42%)
  local copies, waits for them, and re-layouts  114 us (26%)
  loops' own time  43.5 us (10%)
  waiting for transfers between devices  41.9 us (10%)
  matrix products  21 us (5%)
  starting transfers between devices  15.2 us (3%)
  other arithmetic  15.1 us (3%)
    psum x3, blocking collectives, local(): gram_sum, carried = lax.psum((gram_local, carried_local), ('blk', 'lag'))  116 us
    gather x96, local copies, waits for them, and re-layouts  64.4 us
    another operation x1, loops' own time, band_affinity(): lax.scan(one_group, starting, jnp.arange(0, LAGS, lag_group, dtype=jnp.in...  43.5 us
    ppermute x8, waiting for transfers between devices, passed_along(): return lax.ppermute(value, axis, pairs)  41.9 us
    psum x1, blocking collectives, local(): lax.psum((jnp.sum(degree), jnp.dot(vectors, root_degree, precision=highes...  39.9 us
    dynamic_slice x13, local copies, waits for them, and re-layouts, one_group(): lax.dynamic_slice_in_dim(padded, 2 * MAXLAG - 2 * (first_lag + offset), S...  18.6 us
    dot_general x39, matrix products, one_group(): lax.dot_general(shifted, columns, (((1,), (1,)), ((), ())), preferred_ele...  16.5 us
    all_gather x3, blocking collectives, neighbour_vectors(): centre = lax.all_gather(scaled, 'lag', axis=1, tiled=True)  16.2 us
  transfers between devices with their start and end apart: 8, of which 5 were waited for; matrix products, arithmetic and copies ran while one was open for 1% of the time, Pallas kernels for 0%

commit v1 on v0

v1 whole, which is shorter than its diff:
```python
import functools

import jax
import jax.numpy as jnp
from jax import lax
from jax.experimental import pallas as pl
from jax.experimental.pallas import tpu as pltpu
from jax.sharding import PartitionSpec as P

SAMPLES = 1024
MAXLAG = 64
LAGS = 65
OFFBITS = 6
VECTORS = 16
ITERS = 3
COMPS = 3
GROUP = 5
PADDED = SAMPLES + 2 * MAXLAG
SHARPNESS = 64.0
MESH = pl.DeviceIdType.MESH
HIGHEST = lax.Precision.HIGHEST


def kernel(
    nblk,
    nlag,
    own,
    events,
    x_ref,
    shift_ref,
    bits_ref,
    out_ref,
    wall,
    wprev,
    pad,
    shifted,
    columns,
    aff,
    beyond,
    bitbuf,
    dg,
    yn,
    gm,
    wave_send,
    wave_recv,
    bit_send,
    bit_recv,
    aff_send,
    aff_recv,
    far_send,
    far_recv,
    dg_send,
    dg_recv,
    yn_send,
    yn_recv,
    gm_send,
    gm_recv,
):
    b = lax.axis_index("blk")
    me = lax.axis_index("lag")
    width = nlag * own

    def block_at(step):
        return lax.rem(b + step + nblk, nblk)

    def member_at(step):
        return lax.rem(me + step, nlag)

    def remote(src, dst, send, recv, blk, lag):
        return pltpu.make_async_remote_copy(
            src_ref=src,
            dst_ref=dst,
            send_sem=send,
            recv_sem=recv,
            device_id=(blk, lag),
            device_id_type=MESH,
        )

    barrier = pltpu.get_barrier_semaphore()
    partners = [(0, k) for k in range(1, nlag)]
    partners += [(s, k) for s in (1, -1) for k in range(nlag)]
    partners += [(s, 0) for s in range(2, nblk - 1)]
    for step, k in partners:
        pl.semaphore_signal(
            barrier, inc=1, device_id=(block_at(step), member_at(k)), device_id_type=MESH
        )

    x = x_ref[...]
    shift = jnp.broadcast_to(shift_ref[...], x.shape)
    for k in range(OFFBITS):
        moved = pltpu.roll(x, SAMPLES - 2**k, 1)
        x = jnp.where((lax.shift_right_logical(shift, k) & 1) == 1, moved, x)
    lane = lax.broadcasted_iota(jnp.int32, x.shape, 1)
    x = jnp.where(lane + shift < SAMPLES, x, 0.0)
    squares = jnp.sum(x * x, axis=1, keepdims=True)
    energy = squares[0:own] + squares[own : 2 * own] + squares[2 * own : 3 * own]
    scale = lax.rsqrt(energy + 1e-06)
    for c in range(COMPS):
        unit = (x[c * own : (c + 1) * own] * scale).astype(jnp.bfloat16)
        wall[me, :, c * SAMPLES : (c + 1) * SAMPLES] = unit
    bitbuf[0] = bits_ref[...]

    pl.semaphore_wait(barrier, len(partners))

    wave_copies = []
    for k in range(1, nlag):
        wave_copies.append(
            remote(wall.at[me], wall.at[me], wave_send.at[k], wave_recv.at[k], b, member_at(k))
        )
    wave_copies.append(
        remote(wall.at[me], wprev, wave_send.at[0], wave_recv.at[0], block_at(1), me)
    )
    bit_copies = [
        remote(bitbuf.at[0], bitbuf.at[k], bit_send.at[k], bit_recv.at[k], b, member_at(k))
        for k in range(1, nlag)
    ]
    for copy in wave_copies + bit_copies:
        copy.start()

    def place(rows, first):
        for c in range(COMPS):
            piece = rows[:, c * SAMPLES : (c + 1) * SAMPLES].astype(jnp.float32)
            wide = jnp.concatenate([piece, jnp.zeros((own, 2 * MAXLAG), jnp.float32)], 1)
            pad[first : first + own, c * PADDED : (c + 1) * PADDED] = pltpu.roll(
                wide, MAXLAG, 1
            ).astype(pad.dtype)

    place(wall[me], 0)
    for copy in wave_copies:
        copy.wait()
    place(wprev[...], own)
    columns[...] = wall[...].reshape(width, COMPS * SAMPLES).T

    rows = 2 * own

    def one_group(index, running):
        for c in range(COMPS):
            wide = pad[:, c * PADDED : (c + 1) * PADDED]
            for o in range(GROUP):
                moved = wide if o == 0 else pltpu.roll(wide, PADDED - 2 * o, 1)
                shifted[o * rows : (o + 1) * rows, c * SAMPLES : (c + 1) * SAMPLES] = moved[
                    :, :SAMPLES
                ].astype(jnp.bfloat16)
            pad[:, c * PADDED : (c + 1) * PADDED] = pltpu.roll(wide, PADDED - 2 * GROUP, 1)
        scores = jnp.dot(shifted[...], columns[...], preferred_element_type=jnp.float32)
        weights = jnp.exp(SHARPNESS * scores)
        for o in range(GROUP):
            running = running + weights[o * rows : (o + 1) * rows]
        return running

    running = lax.fori_loop(
        0, LAGS // GROUP, one_group, jnp.zeros((rows, width), jnp.float32)
    )
    row_id = lax.broadcasted_iota(jnp.int32, (own, width), 0)
    lane_id = lax.broadcasted_iota(jnp.int32, (own, width), 1)
    aff[me, 1] = jnp.where(lane_id == row_id + me * own, 0.0, running[0:own])
    aff[me, 0] = running[own : 2 * own]

    far_copies = [
        remote(
            aff.at[me, 0], beyond.at[me], far_send.at[k], far_recv.at[k], block_at(-1), member_at(k)
        )
        for k in range(nlag)
    ]
    aff_copies = [
        remote(aff.at[me], aff.at[me], aff_send.at[k], aff_recv.at[k], b, member_at(k))
        for k in range(1, nlag)
    ]
    for copy in far_copies + aff_copies:
        copy.start()
    for copy in bit_copies + far_copies + aff_copies:
        copy.wait()

    before = aff[:, 0].reshape(width, width)
    centre = aff[:, 1].reshape(width, width)
    after = beyond[...].reshape(width, width).T
    degree = jnp.sum(before + centre + after, axis=0, keepdims=True)
    code = bitbuf[0]
    for k in range(1, nlag):
        code = code + bitbuf[k]
    first_row = lax.broadcasted_iota(jnp.int32, (8, width), 0) == 0
    dg[0] = jnp.where(first_row, jnp.broadcast_to(degree, (8, width)), code)
    dg_copies = [
        remote(dg.at[0], dg.at[s], dg_send.at[s], dg_recv.at[s], block_at(s), me)
        for s in range(1, nblk)
    ]
    for copy in dg_copies:
        copy.start()
    for copy in dg_copies:
        copy.wait()

    powers = lax.broadcasted_iota(jnp.int32, (VECTORS, width), 0)
    total_row = jnp.zeros((1, width), jnp.float32)
    proj_lanes = jnp.zeros((VECTORS, width), jnp.float32)
    near = {}
    for s in range(nblk):
        tile = dg[s]
        deg = tile[0:1]
        bits = jnp.broadcast_to(tile[1:2].astype(jnp.int32), (VECTORS, width))
        start = (lax.shift_right_logical(bits, powers) & 1).astype(jnp.float32)
        total_row = total_row + deg
        proj_lanes = proj_lanes + start * jnp.sqrt(deg)
        if s in (0, 1, nblk - 1):
            near[s] = (start, lax.rsqrt(deg), jnp.sqrt(deg))
    total = jnp.sum(total_row, axis=1, keepdims=True)
    projection = jnp.sum(proj_lanes, axis=1, keepdims=True)
    order = (1, 0, nblk - 1)
    inverses = [near[s][1] for s in order]
    vectors = [near[s][0] for s in order]
    inverse, root = near[0][1], near[0][2]
    sub = lax.broadcasted_iota(jnp.int32, (VECTORS, width), 0)
    lane = lax.broadcasted_iota(jnp.int32, (VECTORS, width), 1)

    for it in range(ITERS):
        last = it == ITERS - 1
        applied = jnp.zeros((VECTORS, width), jnp.float32)
        for vector, inv, part in zip(vectors, inverses, (before, centre, after)):
            applied = applied + jnp.dot(
                vector * inv, part, precision=HIGHEST, preferred_element_type=jnp.float32
            )
        deflated = applied * inverse - root * (projection / total)
        yn[it, 0] = deflated
        copies = []
        if not last:
            copies = [
                remote(
                    yn.at[it, 0],
                    yn.at[it, slot],
                    yn_send.at[it, slot],
                    yn_recv.at[it, slot],
                    block_at(step),
                    me,
                )
                for slot, step in ((1, 1), (2, -1))
            ]
            for copy in copies:
                copy.start()
        gram = lax.dot_general(
            deflated,
            deflated,
            (((1,), (1,)), ((), ())),
            precision=HIGHEST,
            preferred_element_type=jnp.float32,
        )
        carried = jnp.sum(deflated * root, axis=1, keepdims=True)
        wide = jnp.concatenate([gram, jnp.zeros((VECTORS, width - VECTORS), jnp.float32)], 1)
        gm[it, 0] = jnp.where(lane == VECTORS, carried, wide)
        gm_copies = [
            remote(
                gm.at[it, 0],
                gm.at[it, s],
                gm_send.at[it, s],
                gm_recv.at[it, s],
                block_at(s),
                me,
            )
            for s in range(1, nblk)
        ]
        for copy in gm_copies:
            copy.start()
        for copy in gm_copies + copies:
            copy.wait()
        table = gm[it, 0]
        for s in range(1, nblk):
            table = table + gm[it, s]
        table = jnp.where(lane < VECTORS, table / events, table)
        tiles = [table, deflated] if last else [table, yn[it, 1], deflated, yn[it, 2]]
        for k in range(VECTORS):
            column = tiles[0][:, k : k + 1]
            r = lax.rsqrt(tiles[0][k : k + 1, k : k + 1])
            factor = jnp.where(sub[:, 0:1] > k, column * r, 0.0)
            updated = []
            for tile in tiles:
                pivot = tile[k : k + 1] * r
                updated.append(jnp.where(sub == k, pivot, tile - factor * pivot))
            tiles = updated
        projection = tiles[0][:, VECTORS : VECTORS + 1]
        vectors = tiles[1:]

    result = jnp.zeros((VECTORS, own), jnp.float32)
    for k in range(nlag):
        result = jnp.where(me == k, vectors[0][:, k * own : (k + 1) * own], result)
    out_ref[...] = result


def local(nblk, nlag, seismograms, onset_shift, start_bits):
    own = seismograms.shape[0]
    width = nlag * own
    events = own * nblk * nlag
    me = lax.axis_index("lag")
    records = jnp.transpose(seismograms, (1, 0, 2)).reshape(COMPS * own, SAMPLES)
    shift = jnp.tile(onset_shift, COMPS)[:, None]
    places = jnp.arange(width, dtype=jnp.int32) // own
    codes = jnp.where(places == me, jnp.tile(start_bits, nlag), 0).astype(jnp.float32)
    codes = jnp.broadcast_to(codes[None, :], (8, width))
    f32, bf16 = jnp.float32, jnp.bfloat16
    dma = pltpu.SemaphoreType.DMA
    flat = COMPS * SAMPLES
    return pl.pallas_call(
        functools.partial(kernel, nblk, nlag, own, events),
        out_shape=jax.ShapeDtypeStruct((VECTORS, own), f32),
        in_specs=[pl.BlockSpec(memory_space=pltpu.VMEM)] * 3,
        out_specs=pl.BlockSpec(memory_space=pltpu.VMEM),
        scratch_shapes=[
            pltpu.VMEM((nlag, own, flat), bf16),
            pltpu.VMEM((own, flat), bf16),
            pltpu.VMEM((2 * own, COMPS * PADDED), PAD_DTYPE),
            pltpu.VMEM((GROUP * 2 * own, flat), bf16),
            pltpu.VMEM((flat, width), bf16),
            pltpu.VMEM((nlag, 2, own, width), f32),
            pltpu.VMEM((nlag, own, width), f32),
            pltpu.VMEM((nlag, 8, width), f32),
            pltpu.VMEM((nblk, 8, width), f32),
            pltpu.VMEM((ITERS, 3, VECTORS, width), f32),
            pltpu.VMEM((ITERS, nblk, VECTORS, width), f32),
            dma((nlag,)),
            dma((nlag,)),
            dma((nlag,)),
            dma((nlag,)),
            dma((nlag,)),
            dma((nlag,)),
            dma((nlag,)),
            dma((nlag,)),
            dma((nblk,)),
            dma((nblk,)),
            dma((ITERS, 3)),
            dma((ITERS, 3)),
            dma((ITERS, nblk)),
            dma((ITERS, nblk)),
        ],
        compiler_params=pltpu.CompilerParams(
            collective_id=0, has_side_effects=True, vmem_limit_bytes=40 * 1024 * 1024
        ),
    )(records, shift, codes)


PAD_DTYPE = jnp.float32


def solution(mesh):
    spec = P(("blk", "lag"))
    return jax.shard_map(
        functools.partial(local, mesh.shape["blk"], mesh.shape["lag"]),
        mesh=mesh,
        in_specs=(P(("blk", "lag"), None, None), spec, spec),
        out_specs=P(None, ("blk", "lag")),
        check_vma=False,
    )
```

time: 435 us -> 60.2 us (0.14)
  blocking collectives: 182 us -> 0 us
  local copies, waits for them, and re-layouts: 114 us -> 3.1 us
  Pallas kernels: 0 us -> 56.9 us
  loops' own time: 43.5 us -> 0 us
  waiting for transfers between devices: 41.9 us -> 0 us
  matrix products: 21 us -> 0 us
  starting transfers between devices: 15.2 us -> 0 us
  other arithmetic: 15.1 us -> 0.01 us
    psum x4 -> x0, blocking collectives: 155 us -> none  [the longest x3 116 us: local(): gram_sum, carried = lax.psum((gram_local, carried_local), ('blk', 'lag'))]
    gather x96 -> x0, local copies, waits for them, and re-layouts: 64.4 us -> none
    pallas_call x0 -> x1, Pallas kernels: none -> 56.9 us  [local(): pl.pallas_call(functools.partial(kernel, nblk, nlag, own, events), out_sh...]
    another operation x2 -> x0, loops' own time: 43.5 us -> none  [the longest x1 43.5 us: band_affinity(): lax.scan(one_group, starting, jnp.arange(0, LAGS, lag_group, dtype=jnp.in...]
    ppermute x8 -> x0, waiting for transfers between devices: 41.9 us -> none  [passed_along(): return lax.ppermute(value, axis, pairs)]
    dynamic_slice x26 -> x0, local copies, waits for them, and re-layouts: 27 us -> none  [the longest x13 18.6 us: one_group(): lax.dynamic_slice_in_dim(padded, 2 * MAXLAG - 2 * (first_lag + offset), S...]
    all_gather x4 -> x0, blocking collectives: 26.3 us -> none  [the longest x3 16.2 us: neighbour_vectors(): centre = lax.all_gather(scaled, 'lag', axis=1, tiled=True)]
    dot_general x48 -> x0, matrix products: 18.2 us -> none  [the longest x39 16.5 us: one_group(): lax.dot_general(shifted, columns, (((1,), (1,)), ((), ())), preferred_ele...]
  transfers between devices with their start and end apart: 8 -> 0, of which waited for: 5 -> 0; matrix products, arithmetic and copies ran while one was open for 1% -> 0% of each run, Pallas kernels for 0% -> 0%
where the time goes in v1:
time: 60.2 us; the launch traced here: 60.1 us
  Pallas kernels  56.9 us (95%)
  local copies, waits for them, and re-layouts  3.1 us (5%)
    pallas_call x1, Pallas kernels, local(): pl.pallas_call(functools.partial(kernel, nblk, nlag, own, events), out_sh...  56.9 us
    unnamed x7, local copies, waits for them, and re-layouts  2.9 us

profile of v1, /device:TPU:0, one launch (start us, length us, event | category | flops | bytes accessed | tf_op | source)
XLA Modules:
  0.0 60.1 jit_solution(15693242637658901547)
XLA Ops:
  0.0 0.0 copy-start.1
  0.0 0.7 %copy-done.1 = s32[32]{0:T(128)S(1)} copy-done((s32[32]{0:T(128)S(1)}, s32[32]{0:T(128)}, u32[]{:S(2)}) %copy-start.1) | copy-done | bytes 152
  0.7 0.0 copy-start.2
  0.7 0.7 %copy-done.2 = s32[32]{0:T(128)S(1)} copy-done((s32[32]{0:T(128)S(1)}, s32[32]{0:T(128)}, u32[]{:S(2)}) %copy-start.2) | copy-done | bytes 152
  1.3 0.1 tile.8
  1.4 0.1 broadcast_in_dim_tile.4.shift_ref
  1.5 0.0 copy-start
  1.5 1.0 %copy-done = f32[32,3,1024]{2,0,1:T(8,128)S(1)} copy-done((f32[32,3,1024]{2,0,1:T(8,128)S(1)}, f32[32,3,1024]{2,0,1:T(8,128)}, u32[]{:S(2)}) %copy-start) | copy-done | bytes 393240
  2.5 56.9 %shard_map.37 = f32[16,32]{1,0:T(8,128)S(1)} custom-call(f32[96,1024]{1,0:T(8,128)S(1)} %bitcast.3, s32[96,1]{1,0:T(8,128)S(1)} %broadcast_in_dim_tile.4.shift_ref, f32[8,128]{1,0:T(8,128)S(1)} %broadcast_in_dim.4.bits_ref), custom_call_target="tpu_custom_call" | custom-call | tf_op jit(solution)/shard_map/pallas_call | solution.py:299
  59.5 0.6 %copy.6 = f32[16,32]{1,0:T(8,128)} copy(f32[16,32]{1,0:T(8,128)S(1)} %shard_map.37) | data formatting | bytes 4096
  (4 shorter events, 0.0 us)
Async XLA Ops:
  0.0 0.7 %copy-start.1 = (s32[32]{0:T(128)S(1)}, s32[32]{0:T(128)}, u32[]{:S(2)}) copy-start(s32[32]{0:T(128)} %param.4) | copy-start | bytes 388
  0.7 0.7 %copy-start.2 = (s32[32]{0:T(128)S(1)}, s32[32]{0:T(128)}, u32[]{:S(2)}) copy-start(s32[32]{0:T(128)} %param.5) | copy-start | bytes 388
  1.5 1.0 %copy-start = (f32[32,3,1024]{2,0,1:T(8,128)S(1)}, f32[32,3,1024]{2,0,1:T(8,128)}, u32[]{:S(2)}) copy-start(f32[32,3,1024]{2,0,1:T(8,128)} %param.3) | copy-start | bytes 1179652

commit v2 on v1

--- a/solution.py
+++ b/solution.py
@@ -14,7 +14,7 @@
 VECTORS = 16
 ITERS = 3
 COMPS = 3
-GROUP = 5
+GROUP = 13
 PADDED = SAMPLES + 2 * MAXLAG
 SHARPNESS = 64.0
 MESH = pl.DeviceIdType.MESH
@@ -26,14 +26,18 @@
     nlag,
     own,
     events,
+    x_hbm,
+    shift_hbm,
+    bits_hbm,
+    out_ref,
     x_ref,
     shift_ref,
     bits_ref,
-    out_ref,
     wall,
     wprev,
     pad,
-    shifted,
+    shifted_own,
+    shifted_before,
     columns,
     aff,
     beyond,
@@ -41,6 +45,7 @@
     dg,
     yn,
     gm,
+    load_sem,
     wave_send,
     wave_recv,
     bit_send,
@@ -76,6 +81,14 @@
             device_id_type=MESH,
         )
 
+    loads = [
+        pltpu.make_async_copy(source, target, load_sem.at[k])
+        for k, (source, target) in enumerate(
+            ((shift_hbm, shift_ref), (bits_hbm, bits_ref), (x_hbm, x_ref))
+        )
+    ]
+    for load in loads:
+        load.start()
     barrier = pltpu.get_barrier_semaphore()
     partners = [(0, k) for k in range(1, nlag)]
     partners += [(s, k) for s in (1, -1) for k in range(nlag)]
@@ -85,8 +98,15 @@
             barrier, inc=1, device_id=(block_at(step), member_at(k)), device_id_type=MESH
         )
 
+    for load in loads:
+        load.wait()
     x = x_ref[...]
-    shift = jnp.broadcast_to(shift_ref[...], x.shape)
+    diagonal = lax.broadcasted_iota(jnp.int32, (own, own), 0) == lax.broadcasted_iota(
+        jnp.int32, (own, own), 1
+    )
+    spread = jnp.broadcast_to(shift_ref[...].astype(jnp.float32), (own, own))
+    column = jnp.sum(jnp.where(diagonal, spread, 0.0), axis=1, keepdims=True).astype(jnp.int32)
+    shift = jnp.concatenate([jnp.broadcast_to(column, (own, SAMPLES))] * COMPS, 0)
     for k in range(OFFBITS):
         moved = pltpu.roll(x, SAMPLES - 2**k, 1)
         x = jnp.where((lax.shift_right_logical(shift, k) & 1) == 1, moved, x)
@@ -98,18 +118,35 @@
     for c in range(COMPS):
         unit = (x[c * own : (c + 1) * own] * scale).astype(jnp.bfloat16)
         wall[me, :, c * SAMPLES : (c + 1) * SAMPLES] = unit
-    bitbuf[0] = bits_ref[...]
+    codes = jnp.concatenate([bits_ref[...].astype(jnp.float32)] * nlag, 1)
+    place_id = lax.broadcasted_iota(jnp.int32, (8, width), 1)
+    mine = (place_id >= me * own) & (place_id < (me + 1) * own)
+    bitbuf[0] = jnp.where(mine, jnp.broadcast_to(codes, (8, width)), 0.0)
 
     pl.semaphore_wait(barrier, len(partners))
 
-    wave_copies = []
-    for k in range(1, nlag):
-        wave_copies.append(
-            remote(wall.at[me], wall.at[me], wave_send.at[k], wave_recv.at[k], b, member_at(k))
-        )
-    wave_copies.append(
-        remote(wall.at[me], wprev, wave_send.at[0], wave_recv.at[0], block_at(1), me)
-    )
+    sibling = me + 1 - 2 * lax.rem(me, 2)
+    across = member_at(2)
+    half = own // 2
+    to_next = remote(wall.at[me], wprev, wave_send.at[0], wave_recv.at[0], block_at(1), me)
+    to_sibling = remote(wall.at[me], wall.at[me], wave_send.at[1], wave_recv.at[1], b, sibling)
+
+    def halves(slot, first_sem, member):
+        return [
+            remote(
+                wall.at[slot, h * half : (h + 1) * half],
+                wall.at[slot, h * half : (h + 1) * half],
+                wave_send.at[first_sem + h],
+                wave_recv.at[first_sem + h],
+                b,
+                member,
+            )
+            for h in range(2)
+        ]
+
+    to_across = halves(me, 2, across)
+    relayed = halves(across, 4, sibling)
+    wave_copies = to_across + [to_next, to_sibling]
     bit_copies = [
         remote(bitbuf.at[0], bitbuf.at[k], bit_send.at[k], bit_recv.at[k], b, member_at(k))
         for k in range(1, nlag)
@@ -117,62 +154,97 @@
     for copy in wave_copies + bit_copies:
         copy.start()
 
-    def place(rows, first):
+    def place(rows):
         for c in range(COMPS):
             piece = rows[:, c * SAMPLES : (c + 1) * SAMPLES].astype(jnp.float32)
             wide = jnp.concatenate([piece, jnp.zeros((own, 2 * MAXLAG), jnp.float32)], 1)
-            pad[first : first + own, c * PADDED : (c + 1) * PADDED] = pltpu.roll(
-                wide, MAXLAG, 1
-            ).astype(pad.dtype)
-
-    place(wall[me], 0)
-    for copy in wave_copies:
-        copy.wait()
-    place(wprev[...], own)
-    columns[...] = wall[...].reshape(width, COMPS * SAMPLES).T
-
-    rows = 2 * own
-
-    def one_group(index, running):
+            pad[:, c * PADDED : (c + 1) * PADDED] = pltpu.roll(wide, MAXLAG, 1).astype(pad.dtype)
+
+    taken = GROUP * own
+
+    def slide(index, target):
         for c in range(COMPS):
             wide = pad[:, c * PADDED : (c + 1) * PADDED]
             for o in range(GROUP):
                 moved = wide if o == 0 else pltpu.roll(wide, PADDED - 2 * o, 1)
-                shifted[o * rows : (o + 1) * rows, c * SAMPLES : (c + 1) * SAMPLES] = moved[
-                    :, :SAMPLES
-                ].astype(jnp.bfloat16)
+                rows = pl.ds(pl.multiple_of(index * taken + o * own, own), own)
+                target[rows, c * SAMPLES : (c + 1) * SAMPLES] = moved[:, :SAMPLES].astype(
+                    jnp.bfloat16
+                )
             pad[:, c * PADDED : (c + 1) * PADDED] = pltpu.roll(wide, PADDED - 2 * GROUP, 1)
-        scores = jnp.dot(shifted[...], columns[...], preferred_element_type=jnp.float32)
+
+    def weigh(index, source, running):
+        rows = pl.ds(pl.multiple_of(index * taken, taken), taken)
+        scores = jnp.dot(source[rows, :], columns[...], preferred_element_type=jnp.float32)
         weights = jnp.exp(SHARPNESS * scores)
         for o in range(GROUP):
-            running = running + weights[o * rows : (o + 1) * rows]
+            running = running + weights[o * own : (o + 1) * own]
         return running
 
-    running = lax.fori_loop(
-        0, LAGS // GROUP, one_group, jnp.zeros((rows, width), jnp.float32)
-    )
+    place(wall[me])
+
+    def slide_own(index, carry):
+        slide(index, shifted_own)
+        return carry
+
+    groups = LAGS // GROUP
+    lax.fori_loop(0, groups, slide_own, 0)
+    for arriving, passing in zip(to_across, relayed):
+        arriving.wait_recv()
+        passing.start()
+    to_next.wait()
+    place(wprev[...])
+    to_sibling.wait()
+    for arriving, passing in zip(to_across, relayed):
+        arriving.wait_send()
+        passing.wait()
+    columns[...] = wall[...].reshape(width, COMPS * SAMPLES).T
+
+    def both(index, running):
+        slide(index, shifted_before)
+        return weigh(index, shifted_own, running)
+
+    zeros = jnp.zeros((own, width), jnp.float32)
+    running = lax.fori_loop(0, groups, both, zeros)
     row_id = lax.broadcasted_iota(jnp.int32, (own, width), 0)
     lane_id = lax.broadcasted_iota(jnp.int32, (own, width), 1)
-    aff[me, 1] = jnp.where(lane_id == row_id + me * own, 0.0, running[0:own])
-    aff[me, 0] = running[own : 2 * own]
-
+    aff[1, me] = jnp.where(lane_id == row_id + me * own, 0.0, running)
+
+    def pieces(part):
+        return [
+            remote(
+                aff.at[part, me],
+                aff.at[part, me],
+                aff_send.at[part, k],
+                aff_recv.at[part, k],
+                b,
+                member_at(k),
+            )
+            for k in range(1, nlag)
+        ]
+
+    centre_copies = pieces(1)
+    for copy in centre_copies:
+        copy.start()
+
+    def only(index, running):
+        return weigh(index, shifted_before, running)
+
+    aff[0, me] = lax.fori_loop(0, groups, only, zeros)
     far_copies = [
         remote(
-            aff.at[me, 0], beyond.at[me], far_send.at[k], far_recv.at[k], block_at(-1), member_at(k)
+            aff.at[0, me], beyond.at[me], far_send.at[k], far_recv.at[k], block_at(-1), member_at(k)
         )
         for k in range(nlag)
     ]
-    aff_copies = [
-        remote(aff.at[me], aff.at[me], aff_send.at[k], aff_recv.at[k], b, member_at(k))
-        for k in range(1, nlag)
-    ]
-    for copy in far_copies + aff_copies:
+    before_copies = pieces(0)
+    for copy in far_copies + before_copies:
         copy.start()
-    for copy in bit_copies + far_copies + aff_copies:
+    for copy in bit_copies + centre_copies + before_copies + far_copies:
         copy.wait()
 
-    before = aff[:, 0].reshape(width, width)
-    centre = aff[:, 1].reshape(width, width)
+    before = aff[0].reshape(width, width)
+    centre = aff[1].reshape(width, width)
     after = beyond[...].reshape(width, width).T
     degree = jnp.sum(before + centre + after, axis=0, keepdims=True)
     code = bitbuf[0]
@@ -287,38 +359,38 @@
     own = seismograms.shape[0]
     width = nlag * own
     events = own * nblk * nlag
-    me = lax.axis_index("lag")
     records = jnp.transpose(seismograms, (1, 0, 2)).reshape(COMPS * own, SAMPLES)
-    shift = jnp.tile(onset_shift, COMPS)[:, None]
-    places = jnp.arange(width, dtype=jnp.int32) // own
-    codes = jnp.where(places == me, jnp.tile(start_bits, nlag), 0).astype(jnp.float32)
-    codes = jnp.broadcast_to(codes[None, :], (8, width))
     f32, bf16 = jnp.float32, jnp.bfloat16
     dma = pltpu.SemaphoreType.DMA
     flat = COMPS * SAMPLES
     return pl.pallas_call(
         functools.partial(kernel, nblk, nlag, own, events),
         out_shape=jax.ShapeDtypeStruct((VECTORS, own), f32),
-        in_specs=[pl.BlockSpec(memory_space=pltpu.VMEM)] * 3,
+        in_specs=[pl.BlockSpec(memory_space=pltpu.HBM)] * 3,
         out_specs=pl.BlockSpec(memory_space=pltpu.VMEM),
         scratch_shapes=[
+            pltpu.VMEM((COMPS * own, SAMPLES), f32),
+            pltpu.VMEM((1, own), jnp.int32),
+            pltpu.VMEM((1, own), jnp.int32),
             pltpu.VMEM((nlag, own, flat), bf16),
             pltpu.VMEM((own, flat), bf16),
-            pltpu.VMEM((2 * own, COMPS * PADDED), PAD_DTYPE),
-            pltpu.VMEM((GROUP * 2 * own, flat), bf16),
+            pltpu.VMEM((own, COMPS * PADDED), PAD_DTYPE),
+            pltpu.VMEM((LAGS * own, flat), bf16),
+            pltpu.VMEM((LAGS * own, flat), bf16),
             pltpu.VMEM((flat, width), bf16),
-            pltpu.VMEM((nlag, 2, own, width), f32),
+            pltpu.VMEM((2, nlag, own, width), f32),
             pltpu.VMEM((nlag, own, width), f32),
             pltpu.VMEM((nlag, 8, width), f32),
             pltpu.VMEM((nblk, 8, width), f32),
             pltpu.VMEM((ITERS, 3, VECTORS, width), f32),
             pltpu.VMEM((ITERS, nblk, VECTORS, width), f32),
+            dma((3,)),
+            dma((6,)),
+            dma((6,)),
             dma((nlag,)),
             dma((nlag,)),
-            dma((nlag,)),
-            dma((nlag,)),
-            dma((nlag,)),
-            dma((nlag,)),
+            dma((2, nlag)),
+            dma((2, nlag)),
             dma((nlag,)),
             dma((nlag,)),
             dma((nblk,)),
@@ -329,9 +401,9 @@
             dma((ITERS, nblk)),
         ],
         compiler_params=pltpu.CompilerParams(
-            collective_id=0, has_side_effects=True, vmem_limit_bytes=40 * 1024 * 1024
+            collective_id=0, has_side_effects=True, vmem_limit_bytes=50 * 1024 * 1024
         ),
-    )(records, shift, codes)
+    )(records, onset_shift[None, :], start_bits[None, :])
 
 
 PAD_DTYPE = jnp.float32

time: 60.2 us -> 53.3 us (0.89)
  Pallas kernels: 56.9 us -> 50.8 us
  local copies, waits for them, and re-layouts: 3.1 us -> 2.27 us
    pallas_call x1, Pallas kernels: 56.9 us -> 50.8 us  [local(): pl.pallas_call(functools.partial(kernel, nblk, nlag, own, events), out_sh...]
    unnamed x7, local copies, waits for them, and re-layouts: 2.9 us -> 2.27 us
where the time goes in v2:
time: 53.3 us; the launch traced here: 53.1 us
  Pallas kernels  50.8 us (95%)
  local copies, waits for them, and re-layouts  2.27 us (4%)
    pallas_call x1, Pallas kernels, local(): pl.pallas_call(functools.partial(kernel, nblk, nlag, own, events), out_sh...  50.8 us
    unnamed x7, local copies, waits for them, and re-layouts  2.27 us

profile of v2, /device:TPU:0, one launch (start us, length us, event | category | flops | bytes accessed | tf_op | source)
XLA Modules:
  0.0 53.1 jit_solution(9379571216933055328)
XLA Ops:
  0.0 0.0 copy-start.1
  0.0 0.0 copy-start.2
  0.0 0.7 %copy-done.1 = s32[32]{0:T(128)S(1)} copy-done((s32[32]{0:T(128)S(1)}, s32[32]{0:T(128)}, u32[]{:S(2)}) %copy-start.1) | copy-done | bytes 152
  0.7 0.0 copy-done.2
  0.7 0.0 copy-start
  0.7 1.0 %copy-done = f32[32,3,1024]{2,0,1:T(8,128)S(1)} copy-done((f32[32,3,1024]{2,0,1:T(8,128)S(1)}, f32[32,3,1024]{2,0,1:T(8,128)}, u32[]{:S(2)}) %copy-start) | copy-done | bytes 393240
  1.7 50.8 %shard_map.37 = f32[16,32]{1,0:T(8,128)S(1)} custom-call(f32[96,1024]{1,0:T(8,128)S(1)} %bitcast.5, s32[1,32]{1,0:T(1,128)S(1)} %bitcast.6, s32[1,32]{1,0:T(1,128)S(1)} %bitcast.7), custom_call_target="tpu_custom_call" | custom-call | tf_op jit(solution)/shard_map/pallas_call | solution.py:366
  52.5 0.6 %copy.5 = f32[16,32]{1,0:T(8,128)} copy(f32[16,32]{1,0:T(8,128)S(1)} %shard_map.37) | data formatting | bytes 4096
Async XLA Ops:
  0.0 0.7 %copy-start.1 = (s32[32]{0:T(128)S(1)}, s32[32]{0:T(128)}, u32[]{:S(2)}) copy-start(s32[32]{0:T(128)} %param.4) | copy-start | bytes 388
  0.0 0.7 %copy-start.2 = (s32[32]{0:T(128)S(1)}, s32[32]{0:T(128)}, u32[]{:S(2)}) copy-start(s32[32]{0:T(128)} %param.5) | copy-start | bytes 388
  0.7 1.0 %copy-start = (f32[32,3,1024]{2,0,1:T(8,128)S(1)}, f32[32,3,1024]{2,0,1:T(8,128)}, u32[]{:S(2)}) copy-start(f32[32,3,1024]{2,0,1:T(8,128)} %param.3) | copy-start | bytes 1179652

commit v3 on v2

--- a/solution.py
+++ b/solution.py
@@ -41,15 +41,15 @@
     columns,
     aff,
     beyond,
-    bitbuf,
+    parts,
     dg,
     yn,
     gm,
     load_sem,
     wave_send,
     wave_recv,
-    bit_send,
-    bit_recv,
+    part_send,
+    part_recv,
     aff_send,
     aff_recv,
     far_send,
@@ -121,7 +121,7 @@
     codes = jnp.concatenate([bits_ref[...].astype(jnp.float32)] * nlag, 1)
     place_id = lax.broadcasted_iota(jnp.int32, (8, width), 1)
     mine = (place_id >= me * own) & (place_id < (me + 1) * own)
-    bitbuf[0] = jnp.where(mine, jnp.broadcast_to(codes, (8, width)), 0.0)
+    codes = jnp.where(mine[0:1], codes, 0.0)
 
     pl.semaphore_wait(barrier, len(partners))
 
@@ -147,11 +147,7 @@
     to_across = halves(me, 2, across)
     relayed = halves(across, 4, sibling)
     wave_copies = to_across + [to_next, to_sibling]
-    bit_copies = [
-        remote(bitbuf.at[0], bitbuf.at[k], bit_send.at[k], bit_recv.at[k], b, member_at(k))
-        for k in range(1, nlag)
-    ]
-    for copy in wave_copies + bit_copies:
+    for copy in wave_copies:
         copy.start()
 
     def place(rows):
@@ -162,19 +158,22 @@
 
     taken = GROUP * own
 
+    def at(first, size):
+        return pl.ds(first if isinstance(first, int) else pl.multiple_of(first, size), size)
+
     def slide(index, target):
         for c in range(COMPS):
             wide = pad[:, c * PADDED : (c + 1) * PADDED]
             for o in range(GROUP):
                 moved = wide if o == 0 else pltpu.roll(wide, PADDED - 2 * o, 1)
-                rows = pl.ds(pl.multiple_of(index * taken + o * own, own), own)
+                rows = at(index * taken + o * own, own)
                 target[rows, c * SAMPLES : (c + 1) * SAMPLES] = moved[:, :SAMPLES].astype(
                     jnp.bfloat16
                 )
             pad[:, c * PADDED : (c + 1) * PADDED] = pltpu.roll(wide, PADDED - 2 * GROUP, 1)
 
     def weigh(index, source, running):
-        rows = pl.ds(pl.multiple_of(index * taken, taken), taken)
+        rows = at(index * taken, taken)
         scores = jnp.dot(source[rows, :], columns[...], preferred_element_type=jnp.float32)
         weights = jnp.exp(SHARPNESS * scores)
         for o in range(GROUP):
@@ -230,7 +229,8 @@
     def only(index, running):
         return weigh(index, shifted_before, running)
 
-    aff[0, me] = lax.fori_loop(0, groups, only, zeros)
+    running = lax.fori_loop(0, groups, only, zeros)
+    aff[0, me] = running
     far_copies = [
         remote(
             aff.at[0, me], beyond.at[me], far_send.at[k], far_recv.at[k], block_at(-1), member_at(k)
@@ -240,18 +240,13 @@
     before_copies = pieces(0)
     for copy in far_copies + before_copies:
         copy.start()
-    for copy in bit_copies + centre_copies + before_copies + far_copies:
-        copy.wait()
-
-    before = aff[0].reshape(width, width)
-    centre = aff[1].reshape(width, width)
-    after = beyond[...].reshape(width, width).T
-    degree = jnp.sum(before + centre + after, axis=0, keepdims=True)
-    code = bitbuf[0]
-    for k in range(1, nlag):
-        code = code + bitbuf[k]
-    first_row = lax.broadcasted_iota(jnp.int32, (8, width), 0) == 0
-    dg[0] = jnp.where(first_row, jnp.broadcast_to(degree, (8, width)), code)
+
+    direct = jnp.sum(aff[1, me] + running, axis=0, keepdims=True)
+    totals = jnp.broadcast_to(jnp.sum(running, axis=1, keepdims=True), (own, own))
+    turned = jnp.sum(jnp.where(diagonal, totals, 0.0), axis=0, keepdims=True)
+    turned = jnp.where(mine[0:1], jnp.concatenate([turned] * nlag, 1), 0.0)
+    sub_id = lax.broadcasted_iota(jnp.int32, (8, width), 0)
+    dg[0] = jnp.where(sub_id == 0, direct, jnp.where(sub_id == 1, turned, codes))
     dg_copies = [
         remote(dg.at[0], dg.at[s], dg_send.at[s], dg_recv.at[s], block_at(s), me)
         for s in range(1, nblk)
@@ -260,15 +255,31 @@
         copy.start()
     for copy in dg_copies:
         copy.wait()
-
+    for s in range(nblk):
+        parts[0, s : s + 1] = dg[s, 0:1] + dg[(s - 1) % nblk, 1:2]
+        parts[0, nblk + s : nblk + s + 1] = dg[s, 2:3]
+    part_copies = [
+        remote(parts.at[0], parts.at[k], part_send.at[k], part_recv.at[k], b, member_at(k))
+        for k in range(1, nlag)
+    ]
+    for copy in part_copies:
+        copy.start()
+    for copy in centre_copies + before_copies + far_copies + part_copies:
+        copy.wait()
+
+    before = aff[0].reshape(width, width)
+    centre = aff[1].reshape(width, width)
+    after = beyond[...].reshape(width, width).T
+    both = parts[0]
+    for k in range(1, nlag):
+        both = both + parts[k]
     powers = lax.broadcasted_iota(jnp.int32, (VECTORS, width), 0)
     total_row = jnp.zeros((1, width), jnp.float32)
     proj_lanes = jnp.zeros((VECTORS, width), jnp.float32)
     near = {}
     for s in range(nblk):
-        tile = dg[s]
-        deg = tile[0:1]
-        bits = jnp.broadcast_to(tile[1:2].astype(jnp.int32), (VECTORS, width))
+        deg = both[s : s + 1]
+        bits = jnp.broadcast_to(both[nblk + s : nblk + s + 1].astype(jnp.int32), (VECTORS, width))
         start = (lax.shift_right_logical(bits, powers) & 1).astype(jnp.float32)
         total_row = total_row + deg
         proj_lanes = proj_lanes + start * jnp.sqrt(deg)
@@ -283,30 +294,27 @@
     sub = lax.broadcasted_iota(jnp.int32, (VECTORS, width), 0)
     lane = lax.broadcasted_iota(jnp.int32, (VECTORS, width), 1)
 
-    for it in range(ITERS):
-        last = it == ITERS - 1
-        applied = jnp.zeros((VECTORS, width), jnp.float32)
-        for vector, inv, part in zip(vectors, inverses, (before, centre, after)):
-            applied = applied + jnp.dot(
-                vector * inv, part, precision=HIGHEST, preferred_element_type=jnp.float32
-            )
+    band = jnp.concatenate([before, centre, after], 0)
+
+    def iterate(it, carry):
+        projection, vectors = carry[0], carry[1:]
+        scaled = jnp.concatenate([v * inv for v, inv in zip(vectors, inverses)], 1)
+        applied = jnp.dot(scaled, band, precision=HIGHEST, preferred_element_type=jnp.float32)
         deflated = applied * inverse - root * (projection / total)
         yn[it, 0] = deflated
-        copies = []
-        if not last:
-            copies = [
-                remote(
-                    yn.at[it, 0],
-                    yn.at[it, slot],
-                    yn_send.at[it, slot],
-                    yn_recv.at[it, slot],
-                    block_at(step),
-                    me,
-                )
-                for slot, step in ((1, 1), (2, -1))
-            ]
-            for copy in copies:
-                copy.start()
+        copies = [
+            remote(
+                yn.at[it, 0],
+                yn.at[it, slot],
+                yn_send.at[it, slot],
+                yn_recv.at[it, slot],
+                block_at(step),
+                me,
+            )
+            for slot, step in ((1, 1), (2, -1))
+        ]
+        for copy in copies:
+            copy.start()
         gram = lax.dot_general(
             deflated,
             deflated,
@@ -336,22 +344,23 @@
         for s in range(1, nblk):
             table = table + gm[it, s]
         table = jnp.where(lane < VECTORS, table / events, table)
-        tiles = [table, deflated] if last else [table, yn[it, 1], deflated, yn[it, 2]]
+        tiles = [table, yn[it, 1], deflated, yn[it, 2]]
         for k in range(VECTORS):
-            column = tiles[0][:, k : k + 1]
-            r = lax.rsqrt(tiles[0][k : k + 1, k : k + 1])
-            factor = jnp.where(sub[:, 0:1] > k, column * r, 0.0)
+            column = jnp.broadcast_to(tiles[0][:, k : k + 1], (VECTORS, width))
+            r = lax.rsqrt(column[k : k + 1])
+            factor = jnp.where(sub > k, column * r, 0.0)
             updated = []
             for tile in tiles:
                 pivot = tile[k : k + 1] * r
                 updated.append(jnp.where(sub == k, pivot, tile - factor * pivot))
             tiles = updated
-        projection = tiles[0][:, VECTORS : VECTORS + 1]
-        vectors = tiles[1:]
+        return (tiles[0][:, VECTORS : VECTORS + 1], *tiles[1:])
+
+    final = lax.fori_loop(0, ITERS, iterate, (projection, *vectors))
 
     result = jnp.zeros((VECTORS, own), jnp.float32)
     for k in range(nlag):
-        result = jnp.where(me == k, vectors[0][:, k * own : (k + 1) * own], result)
+        result = jnp.where(me == k, final[2][:, k * own : (k + 1) * own], result)
     out_ref[...] = result
 
 
@@ -380,7 +389,7 @@
             pltpu.VMEM((flat, width), bf16),
             pltpu.VMEM((2, nlag, own, width), f32),
             pltpu.VMEM((nlag, own, width), f32),
-            pltpu.VMEM((nlag, 8, width), f32),
+            pltpu.VMEM((nlag, 2 * nblk, width), f32),
             pltpu.VMEM((nblk, 8, width), f32),
             pltpu.VMEM((ITERS, 3, VECTORS, width), f32),
             pltpu.VMEM((ITERS, nblk, VECTORS, width), f32),

time: 53.3 us -> 52.9 us (level)
  no operation moved by 1% of the time
where the time goes in v3:
time: 52.9 us; the launch traced here: 52.8 us
  Pallas kernels  50.5 us (95%)
  local copies, waits for them, and re-layouts  2.27 us (4%)
    pallas_call x1, Pallas kernels, local(): pl.pallas_call(functools.partial(kernel, nblk, nlag, own, events), out_sh...  50.5 us
    unnamed x7, local copies, waits for them, and re-layouts  2.27 us

profile of v3, /device:TPU:0, one launch (start us, length us, event | category | flops | bytes accessed | tf_op | source)
XLA Modules:
  0.0 52.8 jit_solution(5874270674028935846)
XLA Ops:
  0.0 0.0 copy-start.1
  0.0 0.0 copy-start.2
  0.0 0.7 %copy-done.1 = s32[32]{0:T(128)S(1)} copy-done((s32[32]{0:T(128)S(1)}, s32[32]{0:T(128)}, u32[]{:S(2)}) %copy-start.1) | copy-done | bytes 152
  0.7 0.0 copy-done.2
  0.7 0.0 copy-start
  0.7 1.0 %copy-done = f32[32,3,1024]{2,0,1:T(8,128)S(1)} copy-done((f32[32,3,1024]{2,0,1:T(8,128)S(1)}, f32[32,3,1024]{2,0,1:T(8,128)}, u32[]{:S(2)}) %copy-start) | copy-done | bytes 393240
  1.7 50.5 %shard_map.37 = f32[16,32]{1,0:T(8,128)S(1)} custom-call(f32[96,1024]{1,0:T(8,128)S(1)} %bitcast.5, s32[1,32]{1,0:T(1,128)S(1)} %bitcast.6, s32[1,32]{1,0:T(1,128)S(1)} %bitcast.7), custom_call_target="tpu_custom_call" | custom-call | tf_op jit(solution)/shard_map/pallas_call | solution.py:375
  52.2 0.6 %copy.5 = f32[16,32]{1,0:T(8,128)} copy(f32[16,32]{1,0:T(8,128)S(1)} %shard_map.37) | data formatting | bytes 4096
Async XLA Ops:
  0.0 0.7 %copy-start.1 = (s32[32]{0:T(128)S(1)}, s32[32]{0:T(128)}, u32[]{:S(2)}) copy-start(s32[32]{0:T(128)} %param.4) | copy-start | bytes 388
  0.0 0.7 %copy-start.2 = (s32[32]{0:T(128)S(1)}, s32[32]{0:T(128)}, u32[]{:S(2)}) copy-start(s32[32]{0:T(128)} %param.5) | copy-start | bytes 388
  0.7 1.0 %copy-start = (f32[32,3,1024]{2,0,1:T(8,128)S(1)}, f32[32,3,1024]{2,0,1:T(8,128)}, u32[]{:S(2)}) copy-start(f32[32,3,1024]{2,0,1:T(8,128)} %param.3) | copy-start | bytes 1179652
